TPU v7x, 32 devices: a whole 2x2x4 slice. The times are simulated.
32 devices in a mesh: grp: 2 (over x), inst: 8 (over z, y), tp: 2 (over core).
Axes of the slice: x: 2, y: 2, z: 4, core: 2. Of those that a mesh axis runs over, the one named last changes fastest.
Arguments:
- key_pool: bfloat16 [640, 8, 128, 128], P(('grp', 'inst'), 'tp'), parts along dimension 0, may hold values from -5 to 5
- value_pool: bfloat16 [640, 8, 128, 128], P(('grp', 'inst'), 'tp'), parts along dimension 0, may hold values from -5 to 5
- block_table: int32 [256, 4], P(('grp', 'inst')), parts along dimension 0, may hold values from 0 to 39, as said below
- lengths: int32 [16, 16], P('grp'), parts along dimension 0, may hold values from 1 to 512, as said below
- pairs: int32 [8, 3], P('grp'), parts along dimension 0, may hold values from 0 to 15, as said below
- queries: bfloat16 [256, 2, 64, 128], P(('grp', 'inst'), None, 'tp'), parts along dimension 0, may hold values from -100 to 100
- new_keys: bfloat16 [256, 2, 8, 128], P(('grp', 'inst'), None, 'tp'), parts along dimension 0, may hold values from -4 to 4
- new_values: bfloat16 [256, 2, 8, 128], P(('grp', 'inst'), None, 'tp'), parts along dimension 0, may hold values from -5 to 5
- guest_queries: bfloat16 [16, 2, 64, 128], P(('grp', 'inst'), None, 'tp'), parts along dimension 0, may hold values from -5 to 5
- guest_new_keys: bfloat16 [16, 2, 8, 128], P(('grp', 'inst'), None, 'tp'), parts along dimension 0, may hold values from -5 to 5
- guest_new_values: bfloat16 [16, 2, 8, 128], P(('grp', 'inst'), None, 'tp'), parts along dimension 0, may hold values from -5 to 5
Outputs:
- attended: bfloat16 [256, 2, 64, 128], P(('grp', 'inst'), None, 'tp'), parts along dimension 0
- guest_keys: bfloat16 [64, 8, 128, 128], P(('grp', 'inst'), 'tp'), parts along dimension 0
- guest_values: bfloat16 [64, 8, 128, 128], P(('grp', 'inst'), 'tp'), parts along dimension 0
There are 2 independent parts, one for each index of `grp`. A program takes and returns all parts, laid end to end along the dimension named above; each array names one. Nothing has to cross between parts.
Inputs may be any that keep to these rules, and one draw needn't show every extreme that they name: `block_table`: entries index the instance's own 40 pool blocks; the blocks that hold positions below a request's length are distinct within an instance. The lengths of one instance together take at most 40 blocks of 128 positions; the largest is reached in every draw. `pairs`: row p concerns instances p and p + 4: one is the source, the other the destination. The moved request's length is at most 510, and equals it in some row of every draw.
All inputs are finite; a program needn't handle non-finite values.
Results may differ from a plain program's by a relative error of at most 0.0049.
Values may be sent and summed in bfloat16 or wider, within the bound.
No kernel may reach another device: no remote copies, remote signals or barrier semaphores. Data moves between devices by JAX's collectives and lax.ppermute only.
A program may use at most 128 MiB of HBM per device.

v0:
```python
import math

import jax
import jax.numpy as jnp
from jax import lax
from jax.sharding import PartitionSpec as P

masked_score = -1e30


def passed_along(value, axis, steps):
    count = lax.axis_size(axis)
    pairs = [(source, (source + steps) % count) for source in range(count)]
    return lax.ppermute(value, axis, pairs)


def attend_batch(key_blocks, value_blocks, length, query_tokens, recent_keys, recent_values):
    row_count, step_count, head_count, head_width = query_tokens.shape
    kv_count = key_blocks.shape[2]
    group_size = head_count // kv_count
    block_count = key_blocks.shape[1]
    block_len = key_blocks.shape[3]
    score_scale = 1.0 / math.sqrt(head_width)
    grouped = query_tokens.reshape(row_count, step_count, kv_count, group_size, head_width)
    context = (
        jnp.einsum("rsgqd,rbgtd->rsgqbt", grouped, key_blocks, preferred_element_type=jnp.float32)
        * score_scale
    )
    position = (
        jnp.arange(block_count, dtype=jnp.int32)[:, None] * block_len
        + jnp.arange(block_len, dtype=jnp.int32)[None, :]
    )
    valid = position[None] < length[:, None, None]
    context = jnp.where(valid[:, None, None, None], context, masked_score)
    recent = (
        jnp.einsum("rsgqd,rtgd->rsgqt", grouped, recent_keys, preferred_element_type=jnp.float32)
        * score_scale
    )
    causal = jnp.arange(step_count)[None, :] <= jnp.arange(step_count)[:, None]
    recent = jnp.where(causal[None, :, None, None, :], recent, masked_score)
    highest = jnp.maximum(jnp.max(context, axis=(4, 5)), jnp.max(recent, axis=4))
    context_exp = jnp.exp(context - highest[..., None, None])
    recent_exp = jnp.exp(recent - highest[..., None])
    denominator = jnp.sum(context_exp, axis=(4, 5)) + jnp.sum(recent_exp, axis=4)
    context_weight = (context_exp / denominator[..., None, None]).astype(jnp.bfloat16)
    recent_weight = (recent_exp / denominator[..., None]).astype(jnp.bfloat16)
    result_sum = jnp.einsum(
        "rsgqbt,rbgtd->rsgqd", context_weight, value_blocks, preferred_element_type=jnp.float32
    )
    result_sum = result_sum + jnp.einsum(
        "rsgqt,rtgd->rsgqd", recent_weight, recent_values, preferred_element_type=jnp.float32
    )
    return result_sum.astype(jnp.bfloat16).reshape(row_count, step_count, head_count, head_width)


def guest_block(blocks, length, recent_rows):
    block_count, kv_count, block_len, head_width = blocks.shape
    position = (
        jnp.arange(block_count, dtype=jnp.int32)[:, None] * block_len
        + jnp.arange(block_len, dtype=jnp.int32)[None, :]
    )
    position = position[:, None, :, None]
    filled = jnp.where(position < length, blocks, jnp.zeros_like(blocks))
    for step_index in range(recent_rows.shape[0]):
        filled = jnp.where(
            position == length + step_index, recent_rows[step_index][None, :, None, :], filled
        )
    return filled


def shards(
    key_pool,
    value_pool,
    block_table,
    lengths,
    pairs,
    queries,
    new_keys,
    new_values,
    guest_queries,
    guest_new_keys,
    guest_new_values,
):
    half_cycle = lax.axis_size("inst") // 2
    own_index = lax.axis_index("inst")
    pair_row = lax.dynamic_index_in_dim(pairs, own_index % half_cycle, 0, keepdims=False)
    source = pair_row[0]
    request = pair_row[1]
    target = pair_row[2]
    own_lengths = lax.dynamic_index_in_dim(lengths, own_index, 0, keepdims=False)
    source_lengths = lax.dynamic_index_in_dim(lengths, source, 0, keepdims=False)
    moved_length = lax.dynamic_index_in_dim(source_lengths, request, 0, keepdims=False)
    key_blocks = key_pool[block_table]
    value_blocks = value_pool[block_table]
    send_keys = lax.dynamic_index_in_dim(key_blocks, request, 0, keepdims=False)
    send_values = lax.dynamic_index_in_dim(value_blocks, request, 0, keepdims=False)
    got_keys, got_values = passed_along((send_keys, send_values), "inst", half_cycle)
    resident = attend_batch(key_blocks, value_blocks, own_lengths, queries, new_keys, new_values)
    served = attend_batch(
        got_keys[None],
        got_values[None],
        moved_length[None],
        guest_queries,
        guest_new_keys,
        guest_new_values,
    )[0]
    moved_result = passed_along(served, "inst", half_cycle)
    row_ids = jnp.arange(own_lengths.shape[0], dtype=jnp.int32)
    replace = (source == own_index) & (row_ids == request)
    attended = jnp.where(replace[:, None, None, None], moved_result[None], resident)
    receiving = target == own_index
    guest_keys = jnp.where(
        receiving, guest_block(got_keys, moved_length, guest_new_keys[0]), jnp.zeros_like(got_keys)
    )
    guest_values = jnp.where(
        receiving,
        guest_block(got_values, moved_length, guest_new_values[0]),
        jnp.zeros_like(got_values),
    )
    return (attended, guest_keys, guest_values)


def solution(mesh):
    return jax.shard_map(
        shards,
        mesh=mesh,
        in_specs=(
            P(("grp", "inst"), "tp", None, None),
            P(("grp", "inst"), "tp", None, None),
            P(("grp", "inst"), None),
            P("grp", None),
            P("grp", None),
            P(("grp", "inst"), None, "tp", None),
            P(("grp", "inst"), None, "tp", None),
            P(("grp", "inst"), None, "tp", None),
            P(("grp", "inst"), None, "tp", None),
            P(("grp", "inst"), None, "tp", None),
            P(("grp", "inst"), None, "tp", None),
        ),
        out_specs=(
            P(("grp", "inst"), None, "tp", None),
            P(("grp", "inst"), "tp", None, None),
            P(("grp", "inst"), "tp", None, None),
        ),
        check_vma=False,
    )
```

profile of v0, /device:TPU:0, one launch (start us, length us, event | category | flops | bytes accessed | tf_op | source)
XLA Modules:
  0.0 69.5 jit_solution(5467316790569947451)
XLA Ops:
  0.7 0.7 %constant_dynamic-slice_fusion.3 = s32[1,3]{1,0:T(1,128)S(1)} fusion(s32[4,3]{1,0:T(4,128)} %param.15, s32[]{:T(128)S(6)} %select_n.92), kind=kLoop, calls=%fused_computation.78 | loop fusion | bytes 28 | tf_op jit(solution)/shard_map/jit(dynamic_index_in_dim)/dynamic_slice | solution.py:86
  1.4 0.6 fusion.44
  3.3 0.7 compare_select_fusion
  4.8 8.0 %gather_fusion.1 = bf16[64,4,128,128]{3,2,1,0:T(8,128)(2,1)} fusion(bf16[40,4,128,128]{3,2,1,0:T(8,128)(2,1)} %param.11, s32[1024]{0:T(1024)S(1)} %pad_clamp_fusion), kind=kCustom, calls=%fused_computation.1 | custom fusion | bytes 16777472 | tf_op jit(solution)/shard_map/gather | solution.py:93
  12.8 1.1 %copy_bitcast_fusion = bf16[4,4,128,128]{3,2,0,1:T(8,128)(2,1)S(1)} fusion(bf16[16,4,4,128,128]{4,3,2,1,0:T(8,128)(2,1)} %bitcast.139, s32[]{:T(128)S(6)} %select_n.94), kind=kLoop, calls=%fused_computation.31 | loop fusion | bytes 1048580 | tf_op jit(solution)/shard_map/jit(dynamic_index_in_dim)/squeeze | solution.py:95
  13.9 4.1 %collective-permute-start.1 = (bf16[4,4,128,128]{3,2,0,1:T(8,128)(2,1)S(1)}, bf16[4,4,128,128]{3,2,0,1:T(8,128)(2,1)S(1)}, u32[]{:S(2)}, u32[]{:S(2)}) collective-permute-start(bf16[4,4,128,128]{3,2,0,1:T(8,128)(2,1)S(1)} %copy_bitcast_fusion), channel_id=1, source_target_pairs={{0,8},{2,10},{4,12},{6,14},{8,0},{10,2},{12,4},{14,6},{1,9},{3,11}... | collective-permute-start | bytes 1572872 | tf_op jit(solution)/shard_map/ppermute | solution.py:14
  18.0 8.0 %gather_fusion = bf16[64,4,128,128]{3,2,1,0:T(8,128)(2,1)} fusion(bf16[40,4,128,128]{3,2,1,0:T(8,128)(2,1)} %param.12, s32[1024]{0:T(1024)S(1)} %pad_clamp_fusion), kind=kCustom, calls=%fused_computation | custom fusion | bytes 16777472 | tf_op jit(solution)/shard_map/gather | solution.py:94
  26.0 1.1 %copy_bitcast_fusion.1 = bf16[4,4,128,128]{3,2,0,1:T(8,128)(2,1)S(1)} fusion(bf16[16,4,4,128,128]{4,3,2,1,0:T(8,128)(2,1)} %bitcast.135, s32[]{:T(128)S(6)} %select_n.94), kind=kLoop, calls=%fused_computation.32 | loop fusion | bytes 1048580 | tf_op jit(solution)/shard_map/jit(dynamic_index_in_dim)/squeeze | solution.py:96
  29.2 0.1 copy.39
  29.3 0.7 fusion.42
  30.7 1.3 %dynamic_slice.22 = s32[1,1]{1,0:T(1,128)} dynamic-slice(s32[8,16]{1,0:T(8,128)} %param.14, s32[]{:T(128)S(6)} %select_n.96, s32[]{:T(128)S(6)} %select_n.97), dynamic_slice_sizes={1,1} | dynamic-slice | bytes 12 | tf_op jit(solution)/shard_map/jit(dynamic_index_in_dim)/dynamic_slice | solution.py:92
  32.6 0.7 %fusion.40 = (pred[4,128]{1,0:T(4,128)(4,1)S(1)}, pred[4,128]{1,0:T(4,128)(4,1)S(1)}, pred[4,128]{1,0:T(4,128)(4,1)S(1)}) fusion(s32[]{:T(128)S(6)} %add.148, s32[4]{0:T(128)S(1)} %iota_multiply_fusion, s32[]{:T(128)} %bitcast.6), kind=kLoop, calls=%fused_computation.67 | loop fusion | flops 2048 | bytes 1560 | tf_op jit(solution)/shard_map/eq | solution.py:66
  33.4 1.3 %fusion.45 = (f32[16,2,4,8]{3,1,2,0:T(2,128)S(1)}, f32[16,2,4,8,2]{3,4,1,2,0:T(2,128)S(1)}) fusion(bf16[16,2,4,128,1]{3,2,1,0,4:T(4,128)(2,1)S(1)} %bitcast.144, pred[2,2]{1,0:T(4,128)(4,1)S(1)} %iota_compare_fusion, bf16[16,2,32,128]{3,2,1,0:T(8,128)(2,1)S(1)} %copy-done), kind=kOutput, calls=%fused_computation.83 | convolution fusion | flops 529408 | bytes 307204 | tf_op jit(solution)/shard_map/rsgqd,rtgd->rsgqt/dot_general | solution.py:36
  34.7 5.9 %bitcast_reduce_fusion = (f32[16,2,4,8]{3,1,2,0:T(2,128)S(1)}, f32[16,4,4,128,2,8]{3,5,4,2,1,0:T(8,128)S(1)}) fusion(pred[16,4,128]{2,1,0:T(4,128)(4,1)S(1)} %broadcast_compare_fusion, bf16[16,4,4,128,128,1]{4,3,2,1,0,5:T(8,128)(2,1)} %bitcast.140, bf16[16,2,32,128]{3,2,1,0:T(8,128)(2,1)S(1)} %copy-done), kind=kOutput, calls=%fused_computation.7 | convolution fusion | flops 135789568 | bytes 10760192 | tf_op jit(solution)/shard_map/rsgqd,rbgtd->rsgqbt/dot_general | solution.py:26
  40.8 0.3 fusion.25
  41.0 0.8 %fusion.5 = f32[16,2,4,8]{3,1,2,0:T(2,128)S(1)} fusion(f32[16,4,4,128,2,8]{3,5,4,2,1,0:T(8,128)S(1)} %get-tuple-element.22, f32[16,2,4,8]{3,1,2,0:T(2,128)S(1)} %max.25, pred[16,4,128]{2,1,0:T(4,128)(4,1)S(1)} %broadcast_compare_fusion), kind=kLoop, calls=%fused_computation.11 | loop fusion | flops 2096128 | bytes 2113536 | tf_op jit(solution)/shard_map/reduce_sum | solution.py:44
  41.9 0.2 convolution_multiply_fusion.2
  42.2 1.6 %fusion.6 = f32[16,2,4,8,128]{4,3,1,2,0:T(8,128)S(1)} fusion(bf16[16,4,4,128,128,1]{4,3,2,1,0,5:T(8,128)(2,1)S(1)} %bitcast.138, f32[16,4,4,128,2,8]{3,5,4,2,1,0:T(8,128)S(1)} %get-tuple-element.22, f32[16,2,4,8]{3,1,2,0:T(2,128)S(1)} %add.146, f32[16,2,4,8]{3,1,2,0:T(2,128)S(1)} %max.25, pred[16,4,128]{2,1,0:T(4,128)(4,1)S(1)} %broadcast_compare_fusion), kind=kOutput, calls=%fused_computation.12 | convolution fusion | flops 136839168 | bytes 11026432 | tf_op jit(solution)/shard_map/rsgqbt,rbgtd->rsgqd/dot_general | solution.py:47
  43.9 0.7 compare_and_fusion
  45.2 0.4 fusion.10
  45.6 7.7 %collective-permute-done.1 = bf16[4,4,128,128]{3,2,0,1:T(8,128)(2,1)S(1)} collective-permute-done((bf16[4,4,128,128]{3,2,0,1:T(8,128)(2,1)S(1)}, bf16[4,4,128,128]{3,2,0,1:T(8,128)(2,1)S(1)}, u32[]{:S(2)}, u32[]{:S(2)}) %collective-permute-start.1) | collective-permute-done | bytes 524320 | tf_op jit(solution)/shard_map/ppermute | solution.py:14
  53.2 0.3 fusion.46
  53.6 0.2 fusion.24
  53.8 0.1 fusion.34
  54.0 0.2 convolution_bitcast_fusion.1
  54.2 9.5 %collective-permute-done = bf16[4,4,128,128]{3,2,0,1:T(8,128)(2,1)S(1)} collective-permute-done((bf16[4,4,128,128]{3,2,0,1:T(8,128)(2,1)S(1)}, bf16[4,4,128,128]{3,2,0,1:T(8,128)(2,1)S(1)}, u32[]{:S(2)}, u32[]{:S(2)}) %collective-permute-start) | collective-permute-done | bytes 524320 | tf_op jit(solution)/shard_map/ppermute | solution.py:14
  63.6 0.2 fusion.18
  64.0 0.4 select_select_fusion
  64.4 0.8 %copy.57 = bf16[4,4,128,128]{3,2,1,0:T(8,128)(2,1)} copy(bf16[4,4,128,128]{3,2,0,1:T(8,128)(2,1)S(1)} %get-tuple-element.13) | data formatting | bytes 1048576
  65.2 0.8 %copy.56 = bf16[4,4,128,128]{3,2,1,0:T(8,128)(2,1)} copy(bf16[4,4,128,128]{3,2,0,1:T(8,128)(2,1)S(1)} %get-tuple-element.14) | data formatting | bytes 1048576
  66.0 2.7 %collective-permute-done.2 = bf16[2,32,128]{2,1,0:T(8,128)(2,1)S(1)} collective-permute-done((bf16[2,32,128]{2,1,0:T(8,128)(2,1)S(1)}, bf16[2,32,128]{2,1,0:T(8,128)(2,1)S(1)}, u32[]{:S(2)}, u32[]{:S(2)}) %collective-permute-start.2) | collective-permute-done | bytes 16416 | tf_op jit(solution)/shard_map/ppermute | solution.py:14
  68.7 0.8 %bitcast_select_fusion = bf16[16,2,32,128]{3,2,1,0:T(8,128)(2,1)} fusion(bf16[16,2,4,8,128]{4,3,1,2,0:T(8,128)(2,1)S(1)} %fusion.10, pred[16]{0:T(512)(128)(4,1)S(1)} %compare_and_fusion, bf16[2,32,128]{2,1,0:T(8,128)(2,1)S(1)} %collective-permute-done.2), kind=kLoop, calls=%fused_computation.36 | loop fusion | flops 131072 | bytes 540688 | tf_op jit(solution)/shard_map/jit(_where)/select_n | solution.py:110
  (34 shorter events, 0.8 us)
Async XLA Ops:
  0.6 32.8 %copy-start = (bf16[16,2,32,128]{3,2,1,0:T(8,128)(2,1)S(1)}, bf16[16,2,32,128]{3,2,1,0:T(8,128)(2,1)}, u32[]{:S(2)}) copy-start(bf16[16,2,32,128]{3,2,1,0:T(8,128)(2,1)} %param.16) | copy-start | bytes 786436
  13.9 19.5 %copy-start.4 = (bf16[16,2,4,128]{3,2,1,0:T(4,128)(2,1)S(1)}, bf16[16,2,4,128]{3,2,1,0:T(4,128)(2,1)}, u32[]{:S(2)}) copy-start(bf16[16,2,4,128]{3,2,1,0:T(4,128)(2,1)} %param.17) | copy-start | bytes 98308
  13.9 39.3 %collective-permute-start.1 = (bf16[4,4,128,128]{3,2,0,1:T(8,128)(2,1)S(1)}, bf16[4,4,128,128]{3,2,0,1:T(8,128)(2,1)S(1)}, u32[]{:S(2)}, u32[]{:S(2)}) collective-permute-start(bf16[4,4,128,128]{3,2,0,1:T(8,128)(2,1)S(1)} %copy_bitcast_fusion), channel_id=1, source_target_pairs={{0,8},{2,10},{4,12},{6,14},{8,0},{10,2},{12,4},{14,6},{1,9},{3,11}... | collective-permute-start | bytes 1572872 | tf_op jit(solution)/shard_map/ppermute | solution.py:14
  27.1 36.5 %collective-permute-start = (bf16[4,4,128,128]{3,2,0,1:T(8,128)(2,1)S(1)}, bf16[4,4,128,128]{3,2,0,1:T(8,128)(2,1)S(1)}, u32[]{:S(2)}, u32[]{:S(2)}) collective-permute-start(bf16[4,4,128,128]{3,2,0,1:T(8,128)(2,1)S(1)} %copy_bitcast_fusion.1), channel_id=1, source_target_pairs={{0,8},{2,10},{4,12},{6,14},{8,0},{10,2},{12,4},{14,6},{1,9},{3,11}... | collective-permute-start | bytes 1572872 | tf_op jit(solution)/shard_map/ppermute | solution.py:14
  34.7 7.4 %slice-start = ((s8[8388608]{0:T(1024)(128)(4,1)}), s8[4194304]{0:T(1024)(128)(4,1)S(1)}, s32[]{:S(2)}) async-start(s8[8388608]{0:T(1024)(128)(4,1)} %bitcast.136), calls=%async_computation | async-start | bytes 8388608
  34.7 7.4 %slice-start.1 = ((s8[8388608]{0:T(1024)(128)(4,1)}), s8[4194304]{0:T(1024)(128)(4,1)S(1)}, s32[]{:S(2)}) async-start(s8[8388608]{0:T(1024)(128)(4,1)} %bitcast.136), calls=%async_computation.1 | async-start | bytes 8388608
  40.7 1.2 %copy-start.1 = (bf16[1,2,32,128]{3,2,1,0:T(8,128)(2,1)S(1)}, bf16[1,2,32,128]{3,2,1,0:T(8,128)(2,1)}, u32[]{:S(2)}) copy-start(bf16[1,2,32,128]{3,2,1,0:T(8,128)(2,1)} %param.19) | copy-start | bytes 49156
  40.7 1.1 %copy-start.3 = (bf16[1,2,4,128]{3,2,1,0:T(4,128)(2,1)S(1)}, bf16[1,2,4,128]{3,2,1,0:T(4,128)(2,1)}, u32[]{:S(2)}) copy-start(bf16[1,2,4,128]{3,2,1,0:T(4,128)(2,1)} %param.20) | copy-start | bytes 6148
  42.2 3.0 %copy-start.2 = (bf16[1,2,4,128]{3,2,1,0:T(4,128)(2,1)S(1)}, bf16[1,2,4,128]{3,2,1,0:T(4,128)(2,1)}, u32[]{:S(2)}) copy-start(bf16[1,2,4,128]{3,2,1,0:T(4,128)(2,1)} %param.21) | copy-start | bytes 6148
  42.2 3.0 %copy-start.5 = (bf16[16,2,4,128]{3,2,1,0:T(4,128)(2,1)S(1)}, bf16[16,2,4,128]{3,2,1,0:T(4,128)(2,1)}, u32[]{:S(2)}) copy-start(bf16[16,2,4,128]{3,2,1,0:T(4,128)(2,1)} %param.18) | copy-start | bytes 98308
  63.9 4.8 %collective-permute-start.2 = (bf16[2,32,128]{2,1,0:T(8,128)(2,1)S(1)}, bf16[2,32,128]{2,1,0:T(8,128)(2,1)S(1)}, u32[]{:S(2)}, u32[]{:S(2)}) collective-permute-start(bf16[2,32,128]{2,1,0:T(8,128)(2,1)S(1)} %bitcast.141), channel_id=1, source_target_pairs={{0,8},{2,10},{4,12},{6,14},{8,0},{10,2},{12,4},{14,6},{1,9},{3,11}... | collective-permute-start | bytes 49160 | tf_op jit(solution)/shard_map/ppermute | solution.py:14
where the time goes:
time: 70 us; the launch traced here: 69.5 us
  local copies, waits for them, and re-layouts  23.5 us (34%)
  waiting for transfers between devices  19.8 us (28%)
  matrix products  10.1 us (14%)
  between operations  6.77 us (10%)
  other arithmetic  5.05 us (7%)
  starting transfers between devices  4.25 us (6%)
    ppermute x3, waiting for transfers between devices, passed_along(): return lax.ppermute(value, axis, pairs)  19.8 us
    gather x1, local copies, waits for them, and re-layouts, shards(): value_blocks = value_pool[block_table]  8.02 us
    gather x1, local copies, waits for them, and re-layouts, shards(): key_blocks = key_pool[block_table]  8.01 us
    dot_general x2, matrix products, attend_batch(): jnp.einsum('rsgqd,rbgtd->rsgqbt', grouped, key_blocks, preferred_element_...  6.26 us
    ppermute x3, starting transfers between devices, passed_along(): return lax.ppermute(value, axis, pairs)  4.25 us
    dot_general x2, matrix products, attend_batch(): jnp.einsum('rsgqbt,rbgtd->rsgqd', context_weight, value_blocks, preferred...  1.88 us
    unnamed x18, local copies, waits for them, and re-layouts  1.71 us
    dot_general x2, matrix products, attend_batch(): jnp.einsum('rsgqd,rtgd->rsgqt', grouped, recent_keys, preferred_element_t...  1.44 us
  transfers between devices with their start and end apart: 3, of which 3 were waited for; matrix products, arithmetic and copies ran while one was open for 38% of the time, Pallas kernels for 0%

commit v1 on v0

--- a/solution.py
+++ b/solution.py
@@ -3,6 +3,8 @@
 import jax
 import jax.numpy as jnp
 from jax import lax
+from jax.experimental import pallas as pl
+from jax.experimental.pallas import tpu as pltpu
 from jax.sharding import PartitionSpec as P
 
 masked_score = -1e30
@@ -68,6 +70,38 @@
     return filled
 
 
+def pick_kernel(blocks, half_cycle, pairs_ref, table_ref, key_ref, value_ref, keys_out, values_out, sems):
+    row = lax.rem(lax.axis_index("inst"), half_cycle)
+    request = pairs_ref[row, 1]
+    copies = []
+    for block in range(blocks):
+        place = table_ref[block, request]
+        copies.append(pltpu.make_async_copy(key_ref.at[place], keys_out.at[block], sems.at[block]))
+        copies.append(
+            pltpu.make_async_copy(value_ref.at[place], values_out.at[block], sems.at[blocks + block])
+        )
+    for copy in copies:
+        copy.start()
+    for copy in copies:
+        copy.wait()
+
+
+def pick_moved(key_pool, value_pool, block_table, pairs, half_cycle):
+    blocks = block_table.shape[1]
+    shape = jax.ShapeDtypeStruct((blocks,) + key_pool.shape[1:], key_pool.dtype)
+    smem = pl.BlockSpec(memory_space=pltpu.SMEM)
+    anywhere = pl.BlockSpec(memory_space=pl.ANY)
+    pool = pl.BlockSpec(memory_space=pltpu.HBM)
+    return pl.pallas_call(
+        lambda *refs: pick_kernel(blocks, half_cycle, *refs),
+        out_shape=(shape, shape),
+        in_specs=[smem, smem, pool, pool],
+        out_specs=(anywhere, anywhere),
+        scratch_shapes=[pltpu.SemaphoreType.DMA((2 * blocks,))],
+        name="pick_moved",
+    )(pairs, block_table.T, key_pool, value_pool)
+
+
 def shards(
     key_pool,
     value_pool,
@@ -83,6 +117,14 @@
 ):
     half_cycle = lax.axis_size("inst") // 2
     own_index = lax.axis_index("inst")
+    send_keys, send_values = pick_moved(key_pool, value_pool, block_table, pairs, half_cycle)
+    got_keys = passed_along(send_keys, "inst", half_cycle)
+    got_values = passed_along(send_values, "inst", half_cycle)
+    guest_tokens = jnp.concatenate([guest_queries, guest_new_keys, guest_new_values], axis=2)
+    moved_tokens = passed_along(guest_tokens, "inst", half_cycle)
+    head_count = queries.shape[2]
+    kv_count = new_keys.shape[2]
+
     pair_row = lax.dynamic_index_in_dim(pairs, own_index % half_cycle, 0, keepdims=False)
     source = pair_row[0]
     request = pair_row[1]
@@ -90,33 +132,21 @@
     own_lengths = lax.dynamic_index_in_dim(lengths, own_index, 0, keepdims=False)
     source_lengths = lax.dynamic_index_in_dim(lengths, source, 0, keepdims=False)
     moved_length = lax.dynamic_index_in_dim(source_lengths, request, 0, keepdims=False)
-    key_blocks = key_pool[block_table]
-    value_blocks = value_pool[block_table]
-    send_keys = lax.dynamic_index_in_dim(key_blocks, request, 0, keepdims=False)
-    send_values = lax.dynamic_index_in_dim(value_blocks, request, 0, keepdims=False)
-    got_keys, got_values = passed_along((send_keys, send_values), "inst", half_cycle)
-    resident = attend_batch(key_blocks, value_blocks, own_lengths, queries, new_keys, new_values)
-    served = attend_batch(
-        got_keys[None],
-        got_values[None],
-        moved_length[None],
-        guest_queries,
-        guest_new_keys,
-        guest_new_values,
-    )[0]
-    moved_result = passed_along(served, "inst", half_cycle)
     row_ids = jnp.arange(own_lengths.shape[0], dtype=jnp.int32)
-    replace = (source == own_index) & (row_ids == request)
-    attended = jnp.where(replace[:, None, None, None], moved_result[None], resident)
+    replace = ((source == own_index) & (row_ids == request))[:, None, None, None]
+    attended = attend_batch(
+        key_pool[block_table],
+        value_pool[block_table],
+        own_lengths,
+        jnp.where(replace, moved_tokens[:, :, :head_count], queries),
+        jnp.where(replace, moved_tokens[:, :, head_count : head_count + kv_count], new_keys),
+        jnp.where(replace, moved_tokens[:, :, head_count + kv_count :], new_values),
+    )
     receiving = target == own_index
-    guest_keys = jnp.where(
-        receiving, guest_block(got_keys, moved_length, guest_new_keys[0]), jnp.zeros_like(got_keys)
-    )
-    guest_values = jnp.where(
-        receiving,
-        guest_block(got_values, moved_length, guest_new_values[0]),
-        jnp.zeros_like(got_values),
-    )
+    guest_length = jnp.where(receiving, moved_length, -guest_new_keys.shape[1])
+    guest_keys = guest_block(got_keys, guest_length, guest_new_keys[0])
+    guest_keys, got_values = lax.optimization_barrier((guest_keys, got_values))
+    guest_values = guest_block(got_values, guest_length, guest_new_values[0])
     return (attended, guest_keys, guest_values)
 
 

time: 70 us -> 89 us (1.27)
  Pallas kernels: 0 us -> 33.8 us
  waiting for transfers between devices: 19.8 us -> 6.45 us
  local copies, waits for them, and re-layouts: 23.5 us -> 20.4 us
  starting transfers between devices: 4.25 us -> 7.03 us
  matrix products: 10.1 us -> 9.19 us
    pallas_call x0 -> x1, Pallas kernels: none -> 33.8 us  [pick_moved(): pl.pallas_call(lambda *refs: pick_kernel(blocks, half_cycle, *refs), out_...]
    ppermute x3, waiting for transfers between devices: 19.8 us -> 6.45 us  [passed_along(): return lax.ppermute(value, axis, pairs)]
    ppermute x3, starting transfers between devices: 4.25 us -> 7.03 us  [passed_along(): return lax.ppermute(value, axis, pairs)]
    squeeze x2 -> x0, local copies, waits for them, and re-layouts: 2.15 us -> none  [the longest x1 1.08 us: shards(): lax.dynamic_index_in_dim(value_blocks, request, 0, keepdims=False)]
    unnamed x18 -> x16, local copies, waits for them, and re-layouts: 1.71 us -> 0.03 us
    select_n x3 -> x4, other arithmetic: 1.86 us -> 2.24 us  [the longest x2 2.13 us: guest_block(): jnp.where(position == length + step_index, recent_rows[step_index][None,...]
    dot_general x2 -> x1, matrix products: 6.26 us -> 5.94 us  [attend_batch(): jnp.einsum('rsgqd,rbgtd->rsgqbt', grouped, key_blocks, preferred_element_...]
    dot_general x2 -> x1, matrix products: 1.88 us -> 1.62 us  [attend_batch(): jnp.einsum('rsgqbt,rbgtd->rsgqd', context_weight, value_blocks, preferred...]
  transfers between devices with their start and end apart: 3 -> 3, of which waited for: 3 -> 1; matrix products, arithmetic and copies ran while one was open for 38% -> 37% of each run, Pallas kernels for 0% -> 38%
where the time goes in v1:
time: 89 us; the launch traced here: 88.6 us
  Pallas kernels  33.8 us (38%)
  local copies, waits for them, and re-layouts  20.4 us (23%)
  matrix products  9.19 us (10%)
  starting transfers between devices  7.03 us (8%)
  between operations  6.58 us (7%)
  waiting for transfers between devices  6.45 us (7%)
  other arithmetic  5.16 us (6%)
    pallas_call x1, Pallas kernels, pick_moved(): pl.pallas_call(lambda *refs: pick_kernel(blocks, half_cycle, *refs), out_...  33.8 us
    gather x1, local copies, waits for them, and re-layouts, shards(): value_pool[block_table]  8.06 us
    gather x1, local copies, waits for them, and re-layouts, shards(): key_pool[block_table]  8.04 us
    ppermute x3, starting transfers between devices, passed_along(): return lax.ppermute(value, axis, pairs)  7.03 us
    ppermute x3, waiting for transfers between devices, passed_along(): return lax.ppermute(value, axis, pairs)  6.45 us
    dot_general x1, matrix products, attend_batch(): jnp.einsum('rsgqd,rbgtd->rsgqbt', grouped, key_blocks, preferred_element_...  5.94 us
    select_n x2, other arithmetic, guest_block(): jnp.where(position == length + step_index, recent_rows[step_index][None,...  2.13 us
  transfers between devices with their start and end apart: 3, of which 1 were waited for; matrix products, arithmetic and copies ran while one was open for 37% of the time, Pallas kernels for 38%

profile of v1, /device:TPU:0, one launch (start us, length us, event | category | flops | bytes accessed | tf_op | source)
XLA Modules:
  0.0 88.6 jit_solution(3437606097662058397)
XLA Ops:
  0.6 0.8 pad_maximum_fusion
  1.4 4.0 %collective-permute-start = (bf16[1,2,40,128]{3,2,1,0:T(8,128)(2,1)S(1)}, bf16[1,2,40,128]{3,2,1,0:T(8,128)(2,1)S(1)}, u32[]{:S(2)}, u32[]{:S(2)}) collective-permute-start(bf16[1,2,40,128]{3,2,1,0:T(8,128)(2,1)S(1)} %pad_maximum_fusion), channel_id=1, source_target_pairs={{0,8},{2,10},{4,12},{6,14},{8,0},{10,2},{12,4},{14,6},{1,9},{3,11}... | collective-permute-start | bytes 61448 | tf_op jit(solution)/shard_map/ppermute | solution.py:16
  5.4 33.8 %pick_moved.1 = (bf16[4,4,128,128]{3,2,1,0:T(8,128)(2,1)}, bf16[4,4,128,128]{3,2,1,0:T(8,128)(2,1)}) custom-call(s32[4,3]{1,0:T(4,128)} %refs_0_.1, s32[4,16]{1,0:T(4,128)} %bitcast.64, bf16[40,4,128,128]{3,2,1,0:T(8,128)(2,1)} %refs_2_.1, bf16[40,4,128,128]{3,2,1,0:T(8,128)(2,1)} %refs_3_.1), custom_call_target="tpu_custom_call" | custom-call | tf_op jit(solution)/shard_map/pick_moved/pallas_call | solution.py:95
  39.3 0.1 collective-permute-start.1
  39.4 2.9 %collective-permute-start.2 = (bf16[4,4,128,128]{3,2,1,0:T(8,128)(2,1)}, bf16[4,4,128,128]{3,2,1,0:T(8,128)(2,1)S(1)}, u32[]{:S(2)}, u32[]{:S(2)}) collective-permute-start(bf16[4,4,128,128]{3,2,1,0:T(8,128)(2,1)} %get-tuple-element.8), channel_id=1, source_target_pairs={{0,8},{2,10},{4,12},{6,14},{8,0},{10,2},{12,4},{14,6},{1,9},{3,11}... | collective-permute-start | bytes 1572872 | tf_op jit(solution)/shard_map/ppermute | solution.py:16
  42.3 0.7 constant_dynamic-slice_fusion
  42.9 0.7 fusion.26
  47.5 0.1 iota_add_fusion
  47.5 0.7 dynamic-slice_bitcast_fusion
  49.5 1.3 %dynamic_slice.15 = s32[1,1]{1,0:T(1,128)} dynamic-slice(s32[8,16]{1,0:T(8,128)} %param.14, s32[]{:T(128)S(6)} %select_n.87, s32[]{:T(128)S(6)} %select_n.89), dynamic_slice_sizes={1,1} | dynamic-slice | bytes 12 | tf_op jit(solution)/shard_map/jit(dynamic_index_in_dim)/dynamic_slice | solution.py:134
  51.4 0.1 fusion.25
  51.5 0.1 copy.22
  51.6 0.1 reshape.162
  51.7 0.1 broadcast_compare_fusion
  51.8 0.7 compare_and_fusion
  52.5 8.0 %gather_fusion.1 = bf16[64,4,128,128]{3,2,1,0:T(8,128)(2,1)} fusion(bf16[40,4,128,128]{3,2,1,0:T(8,128)(2,1)} %refs_2_.1, s32[1024]{0:T(1024)S(1)} %pad_clamp_fusion), kind=kCustom, calls=%fused_computation.1 | custom fusion | bytes 16777472 | tf_op jit(solution)/shard_map/gather | solution.py:138
  60.5 8.1 %gather_fusion = bf16[64,4,128,128]{3,2,1,0:T(8,128)(2,1)} fusion(bf16[40,4,128,128]{3,2,1,0:T(8,128)(2,1)} %refs_3_.1, s32[1024]{0:T(1024)S(1)} %pad_clamp_fusion), kind=kCustom, calls=%fused_computation | custom fusion | bytes 16777472 | tf_op jit(solution)/shard_map/gather | solution.py:139
  68.6 0.0 collective-permute-done
  68.6 0.1 fusion.17
  68.7 0.1 select_bitcast_fusion
  68.8 1.3 %fusion.27 = (f32[16,2,4,8]{3,1,2,0:T(2,128)S(1)}, f32[16,2,4,8,2]{3,4,1,2,0:T(2,128)S(1)}) fusion(bf16[16,2,4,8,128]{4,3,2,1,0:T(8,128)(2,1)S(1)} %get-tuple-element.11, bf16[16,2,4,128,1]{3,2,1,0,4:T(4,128)(2,1)S(1)} %get-tuple-element.26, pred[2,2]{1,0:T(4,128)(4,1)S(1)} %iota_compare_fusion), kind=kOutput, calls=%fused_computation.58 | convolution fusion | flops 529408 | bytes 307204 | tf_op jit(solution)/shard_map/rsgqd,rtgd->rsgqt/dot_general | solution.py:38
  70.1 0.0 slice-start.1
  70.1 5.9 %bitcast_reduce_fusion = (f32[16,2,4,8]{3,1,2,0:T(2,128)S(1)}, f32[16,4,4,128,2,8]{3,5,4,2,1,0:T(8,128)S(1)}) fusion(pred[16,4,128]{2,1,0:T(4,128)(4,1)S(1)} %broadcast_compare_fusion, bf16[16,2,4,8,128,1]{4,3,2,1,0,5:T(8,128)(2,1)S(1)} %get-tuple-element.12, bf16[16,4,4,128,128,1]{4,3,2,1,0,5:T(8,128)(2,1)} %bitcast.62), kind=kOutput, calls=%fused_computation.7 | convolution fusion | flops 135789568 | bytes 10760192 | tf_op jit(solution)/shard_map/rsgqd,rbgtd->rsgqbt/dot_general | solution.py:28
  76.1 0.3 fusion.18
  76.4 0.8 fusion.5
  77.3 1.6 %fusion.6 = f32[16,4,128,2,8]{2,4,3,1,0:T(8,128)S(1)} fusion(bf16[16,4,4,128,128,1]{4,3,2,1,0,5:T(8,128)(2,1)S(1)} %bitcast.61, f32[16,4,4,128,2,8]{3,5,4,2,1,0:T(8,128)S(1)} %get-tuple-element.28, f32[16,2,4,8]{3,1,2,0:T(2,128)S(1)} %add.110, f32[16,2,4,8]{3,1,2,0:T(2,128)S(1)} %max.11, pred[16,4,128]{2,1,0:T(4,128)(4,1)S(1)} %broadcast_compare_fusion), kind=kOutput, calls=%fused_computation.12 | convolution fusion | flops 136839168 | bytes 11026432 | tf_op jit(solution)/shard_map/rsgqbt,rbgtd->rsgqd/dot_general | solution.py:49
  78.9 0.3 fusion.10
  79.3 0.7 copy.72
  80.0 0.0 collective-permute-done.1
  80.0 1.1 %select_select_fusion.1 = bf16[4,4,128,128]{3,2,1,0:T(8,128)(2,1)} fusion(bf16[4,4,128,128]{3,2,1,0:T(8,128)(2,1)S(1)} %collective-permute-done.1, pred[4,128]{1,0:T(4,128)(4,1)S(1)} %get-tuple-element.20, pred[4,128]{1,0:T(4,128)(4,1)S(1)} %get-tuple-element.21, pred[4,128]{1,0:T(4,128)(4,1)S(1)} %get-tuple-element.19, ...), kind=kLoop, calls=%fused_computation.21 | loop fusion | flops 786432 | bytes 1052160 | tf_op jit(solution)/shard_map/jit(_where)/select_n | solution.py:67
  81.1 6.4 %collective-permute-done.2 = bf16[4,4,128,128]{3,2,1,0:T(8,128)(2,1)S(1)} collective-permute-done((bf16[4,4,128,128]{3,2,1,0:T(8,128)(2,1)}, bf16[4,4,128,128]{3,2,1,0:T(8,128)(2,1)S(1)}, u32[]{:S(2)}, u32[]{:S(2)}) %collective-permute-start.2) | collective-permute-done | bytes 524320 | tf_op jit(solution)/shard_map/ppermute | solution.py:16
  87.5 1.1 %select_select_fusion = bf16[4,4,128,128]{3,2,1,0:T(8,128)(2,1)} fusion(bf16[4,4,128,128]{3,2,1,0:T(8,128)(2,1)S(1)} %collective-permute-done.2, pred[4,128]{1,0:T(4,128)(4,1)S(1)} %get-tuple-element.20, pred[4,128]{1,0:T(4,128)(4,1)S(1)} %get-tuple-element.21, pred[4,128]{1,0:T(4,128)(4,1)S(1)} %get-tuple-element.19, ...), kind=kLoop, calls=%fused_computation.20 | loop fusion | flops 786432 | bytes 1052160 | tf_op jit(solution)/shard_map/jit(_where)/select_n | solution.py:67
  (26 shorter events, 0.1 us)
Async XLA Ops:
  1.4 67.2 %collective-permute-start = (bf16[1,2,40,128]{3,2,1,0:T(8,128)(2,1)S(1)}, bf16[1,2,40,128]{3,2,1,0:T(8,128)(2,1)S(1)}, u32[]{:S(2)}, u32[]{:S(2)}) collective-permute-start(bf16[1,2,40,128]{3,2,1,0:T(8,128)(2,1)S(1)} %pad_maximum_fusion), channel_id=1, source_target_pairs={{0,8},{2,10},{4,12},{6,14},{8,0},{10,2},{12,4},{14,6},{1,9},{3,11}... | collective-permute-start | bytes 61448 | tf_op jit(solution)/shard_map/ppermute | solution.py:16
  5.4 40.0 %copy-start.3 = (s32[16,4]{0,1:T(4,128)S(1)}, s32[16,4]{0,1:T(4,128)}, u32[]{:S(2)}) copy-start(s32[16,4]{0,1:T(4,128)} %param.13) | copy-start | bytes 772
  5.4 40.1 %copy-start.4 = (bf16[1,2,4,128]{3,2,1,0:T(4,128)(2,1)S(1)}, bf16[1,2,4,128]{3,2,1,0:T(4,128)(2,1)}, u32[]{:S(2)}) copy-start(bf16[1,2,4,128]{3,2,1,0:T(4,128)(2,1)} %param.20) | copy-start | bytes 6148
  5.4 40.1 %copy-start.5 = (bf16[1,2,4,128]{3,2,1,0:T(4,128)(2,1)S(1)}, bf16[1,2,4,128]{3,2,1,0:T(4,128)(2,1)}, u32[]{:S(2)}) copy-start(bf16[1,2,4,128]{3,2,1,0:T(4,128)(2,1)} %param.21) | copy-start | bytes 6148
  39.3 40.7 %collective-permute-start.1 = (bf16[4,4,128,128]{3,2,1,0:T(8,128)(2,1)}, bf16[4,4,128,128]{3,2,1,0:T(8,128)(2,1)S(1)}, u32[]{:S(2)}, u32[]{:S(2)}) collective-permute-start(bf16[4,4,128,128]{3,2,1,0:T(8,128)(2,1)} %get-tuple-element.7), channel_id=1, source_target_pairs={{0,8},{2,10},{4,12},{6,14},{8,0},{10,2},{12,4},{14,6},{1,9},{3,11}... | collective-permute-start | bytes 1572872 | tf_op jit(solution)/shard_map/ppermute | solution.py:16
  39.4 48.2 %collective-permute-start.2 = (bf16[4,4,128,128]{3,2,1,0:T(8,128)(2,1)}, bf16[4,4,128,128]{3,2,1,0:T(8,128)(2,1)S(1)}, u32[]{:S(2)}, u32[]{:S(2)}) collective-permute-start(bf16[4,4,128,128]{3,2,1,0:T(8,128)(2,1)} %get-tuple-element.8), channel_id=1, source_target_pairs={{0,8},{2,10},{4,12},{6,14},{8,0},{10,2},{12,4},{14,6},{1,9},{3,11}... | collective-permute-start | bytes 1572872 | tf_op jit(solution)/shard_map/ppermute | solution.py:16
  60.5 8.1 %copy-start = (bf16[16,2,32,128]{3,2,1,0:T(8,128)(2,1)S(1)}, bf16[16,2,32,128]{3,2,1,0:T(8,128)(2,1)}, u32[]{:S(2)}) copy-start(bf16[16,2,32,128]{3,2,1,0:T(8,128)(2,1)} %param.16) | copy-start | bytes 786436
  60.5 8.2 %copy-start.1 = (bf16[16,2,4,128]{3,2,1,0:T(4,128)(2,1)S(1)}, bf16[16,2,4,128]{3,2,1,0:T(4,128)(2,1)}, u32[]{:S(2)}) copy-start(bf16[16,2,4,128]{3,2,1,0:T(4,128)(2,1)} %param.18) | copy-start | bytes 98308
  60.5 8.2 %copy-start.2 = (bf16[16,2,4,128]{3,2,1,0:T(4,128)(2,1)S(1)}, bf16[16,2,4,128]{3,2,1,0:T(4,128)(2,1)}, u32[]{:S(2)}) copy-start(bf16[16,2,4,128]{3,2,1,0:T(4,128)(2,1)} %param.17) | copy-start | bytes 98308
  70.1 7.1 %slice-start = ((s8[8388608]{0:T(1024)(128)(4,1)}), s8[4194304]{0:T(1024)(128)(4,1)S(1)}, s32[]{:S(2)}) async-start(s8[8388608]{0:T(1024)(128)(4,1)} %bitcast.59), calls=%async_computation | async-start | bytes 8388608
  70.1 7.1 %slice-start.1 = ((s8[8388608]{0:T(1024)(128)(4,1)}), s8[4194304]{0:T(1024)(128)(4,1)S(1)}, s32[]{:S(2)}) async-start(s8[8388608]{0:T(1024)(128)(4,1)} %bitcast.59), calls=%async_computation.1 | async-start | bytes 8388608

commit v2 on v1

--- a/solution.py
+++ b/solution.py
@@ -90,13 +90,13 @@
     blocks = block_table.shape[1]
     shape = jax.ShapeDtypeStruct((blocks,) + key_pool.shape[1:], key_pool.dtype)
     smem = pl.BlockSpec(memory_space=pltpu.SMEM)
-    anywhere = pl.BlockSpec(memory_space=pl.ANY)
+    vmem = pl.BlockSpec(memory_space=pltpu.VMEM)
     pool = pl.BlockSpec(memory_space=pltpu.HBM)
     return pl.pallas_call(
         lambda *refs: pick_kernel(blocks, half_cycle, *refs),
         out_shape=(shape, shape),
         in_specs=[smem, smem, pool, pool],
-        out_specs=(anywhere, anywhere),
+        out_specs=(vmem, vmem),
         scratch_shapes=[pltpu.SemaphoreType.DMA((2 * blocks,))],
         name="pick_moved",
     )(pairs, block_table.T, key_pool, value_pool)

time: 89 us -> 58.4 us (0.66)
  Pallas kernels: 33.8 us -> 3.19 us
    pallas_call x1, Pallas kernels: 33.8 us -> 3.19 us  [pick_moved(): pl.pallas_call(lambda *refs: pick_kernel(blocks, half_cycle, *refs), out_...]
  transfers between devices with their start and end apart: 3 -> 3, of which waited for: 1 -> 1; matrix products, arithmetic and copies ran while one was open for 37% -> 57% of each run, Pallas kernels for 38% -> 6%
where the time goes in v2:
time: 58.4 us; the launch traced here: 58 us
  local copies, waits for them, and re-layouts  20.4 us (35%)
  matrix products  9.19 us (16%)
  starting transfers between devices  7.03 us (12%)
  between operations  6.58 us (11%)
  waiting for transfers between devices  6.45 us (11%)
  other arithmetic  5.16 us (9%)
  Pallas kernels  3.19 us (5%)
    gather x1, local copies, waits for them, and re-layouts, shards(): value_pool[block_table]  8.06 us
    gather x1, local copies, waits for them, and re-layouts, shards(): key_pool[block_table]  8.04 us
    ppermute x3, starting transfers between devices, passed_along(): return lax.ppermute(value, axis, pairs)  7.03 us
    ppermute x3, waiting for transfers between devices, passed_along(): return lax.ppermute(value, axis, pairs)  6.45 us
    dot_general x1, matrix products, attend_batch(): jnp.einsum('rsgqd,rbgtd->rsgqbt', grouped, key_blocks, preferred_element_...  5.94 us
    pallas_call x1, Pallas kernels, pick_moved(): pl.pallas_call(lambda *refs: pick_kernel(blocks, half_cycle, *refs), out_...  3.19 us
    select_n x2, other arithmetic, guest_block(): jnp.where(position == length + step_index, recent_rows[step_index][None,...  2.13 us
    dot_general x1, matrix products, attend_batch(): jnp.einsum('rsgqbt,rbgtd->rsgqd', context_weight, value_blocks, preferred...  1.62 us
  transfers between devices with their start and end apart: 3, of which 1 were waited for; matrix products, arithmetic and copies ran while one was open for 57% of the time, Pallas kernels for 6%

profile of v2, /device:TPU:0, one launch (start us, length us, event | category | flops | bytes accessed | tf_op | source)
XLA Modules:
  0.0 58.0 jit_solution(7980000134618931808)
XLA Ops:
  0.6 0.8 %pad_maximum_fusion = bf16[1,2,40,128]{3,2,1,0:T(8,128)(2,1)S(1)} fusion(bf16[1,2,4,128]{3,2,1,0:T(4,128)(2,1)} %param.21, bf16[1,2,4,128]{3,2,1,0:T(4,128)(2,1)} %param.20, bf16[1,2,32,128]{3,2,1,0:T(8,128)(2,1)} %param.19), kind=kLoop, calls=%fused_computation.37 | loop fusion | flops 61440 | bytes 40960 | tf_op jit(solution)/shard_map/concatenate | solution.py:123
  1.4 4.0 %collective-permute-start = (bf16[1,2,40,128]{3,2,1,0:T(8,128)(2,1)S(1)}, bf16[1,2,40,128]{3,2,1,0:T(8,128)(2,1)S(1)}, u32[]{:S(2)}, u32[]{:S(2)}) collective-permute-start(bf16[1,2,40,128]{3,2,1,0:T(8,128)(2,1)S(1)} %pad_maximum_fusion), channel_id=1, source_target_pairs={{0,8},{2,10},{4,12},{6,14},{8,0},{10,2},{12,4},{14,6},{1,9},{3,11}... | collective-permute-start | bytes 61448 | tf_op jit(solution)/shard_map/ppermute | solution.py:16
  5.4 3.2 %pick_moved.1 = (bf16[4,4,128,128]{3,2,1,0:T(8,128)(2,1)}, bf16[4,4,128,128]{3,2,1,0:T(8,128)(2,1)}) custom-call(s32[4,3]{1,0:T(4,128)} %refs_0_.1, s32[4,16]{1,0:T(4,128)} %bitcast.64, bf16[40,4,128,128]{3,2,1,0:T(8,128)(2,1)} %refs_2_.1, bf16[40,4,128,128]{3,2,1,0:T(8,128)(2,1)} %refs_3_.1), custom_call_target="tpu_custom_call" | custom-call | tf_op jit(solution)/shard_map/pick_moved/pallas_call | solution.py:95
  8.6 0.1 collective-permute-start.1
  8.7 2.9 %collective-permute-start.2 = (bf16[4,4,128,128]{3,2,1,0:T(8,128)(2,1)}, bf16[4,4,128,128]{3,2,1,0:T(8,128)(2,1)S(1)}, u32[]{:S(2)}, u32[]{:S(2)}) collective-permute-start(bf16[4,4,128,128]{3,2,1,0:T(8,128)(2,1)} %get-tuple-element.8), channel_id=1, source_target_pairs={{0,8},{2,10},{4,12},{6,14},{8,0},{10,2},{12,4},{14,6},{1,9},{3,11}... | collective-permute-start | bytes 1572872 | tf_op jit(solution)/shard_map/ppermute | solution.py:16
  11.6 0.7 %constant_dynamic-slice_fusion = s32[1,3]{1,0:T(1,128)S(1)} fusion(s32[4,3]{1,0:T(4,128)} %refs_0_.1, s32[]{:T(128)S(6)} %select_n.79), kind=kLoop, calls=%fused_computation.56 | loop fusion | bytes 28 | tf_op jit(solution)/shard_map/jit(dynamic_index_in_dim)/dynamic_slice | solution.py:128
  12.3 0.7 %fusion.26 = (s32[1,1]{1,0:T(1,128)}, s32[1,1]{1,0:T(1,128)}, s32[1,1]{1,0:T(1,128)}) fusion(s32[1,3]{1,0:T(1,128)S(1)} %constant_dynamic-slice_fusion), kind=kLoop, calls=%fused_computation.57 | loop fusion | bytes 24 | tf_op jit(solution)/shard_map/slice | solution.py:131
  16.9 0.1 iota_add_fusion
  16.9 0.7 %dynamic-slice_bitcast_fusion = s32[16]{0:T(128)S(1)} fusion(s32[8,16]{1,0:T(8,128)} %param.14, s32[]{:T(128)S(6)} %select_n.77), kind=kLoop, calls=%fused_computation.54 | loop fusion | bytes 132 | tf_op jit(solution)/shard_map/lt | solution.py:35
  18.9 1.3 %dynamic_slice.15 = s32[1,1]{1,0:T(1,128)} dynamic-slice(s32[8,16]{1,0:T(8,128)} %param.14, s32[]{:T(128)S(6)} %select_n.87, s32[]{:T(128)S(6)} %select_n.89), dynamic_slice_sizes={1,1} | dynamic-slice | bytes 12 | tf_op jit(solution)/shard_map/jit(dynamic_index_in_dim)/dynamic_slice | solution.py:134
  20.8 0.1 fusion.25
  20.9 0.1 copy.22
  21.0 0.1 reshape.162
  21.1 0.1 broadcast_compare_fusion
  21.2 0.7 %compare_and_fusion = pred[16]{0:T(512)(128)(4,1)S(1)} fusion(pred[]{:T(512)S(6)} %eq.44, s32[]{:T(128)} %bitcast.6), kind=kLoop, calls=%fused_computation.48 | loop fusion | flops 32 | bytes 21 | tf_op jit(solution)/shard_map/and | solution.py:136
  21.8 8.0 %gather_fusion.1 = bf16[64,4,128,128]{3,2,1,0:T(8,128)(2,1)} fusion(bf16[40,4,128,128]{3,2,1,0:T(8,128)(2,1)} %refs_2_.1, s32[1024]{0:T(1024)S(1)} %pad_clamp_fusion), kind=kCustom, calls=%fused_computation.1 | custom fusion | bytes 16777472 | tf_op jit(solution)/shard_map/gather | solution.py:138
  29.9 8.1 %gather_fusion = bf16[64,4,128,128]{3,2,1,0:T(8,128)(2,1)} fusion(bf16[40,4,128,128]{3,2,1,0:T(8,128)(2,1)} %refs_3_.1, s32[1024]{0:T(1024)S(1)} %pad_clamp_fusion), kind=kCustom, calls=%fused_computation | custom fusion | bytes 16777472 | tf_op jit(solution)/shard_map/gather | solution.py:139
  37.9 0.0 collective-permute-done
  38.0 0.1 fusion.17
  38.1 0.1 select_bitcast_fusion
  38.2 1.3 %fusion.27 = (f32[16,2,4,8]{3,1,2,0:T(2,128)S(1)}, f32[16,2,4,8,2]{3,4,1,2,0:T(2,128)S(1)}) fusion(bf16[16,2,4,8,128]{4,3,2,1,0:T(8,128)(2,1)S(1)} %get-tuple-element.11, bf16[16,2,4,128,1]{3,2,1,0,4:T(4,128)(2,1)S(1)} %get-tuple-element.26, pred[2,2]{1,0:T(4,128)(4,1)S(1)} %iota_compare_fusion), kind=kOutput, calls=%fused_computation.58 | convolution fusion | flops 529408 | bytes 307204 | tf_op jit(solution)/shard_map/rsgqd,rtgd->rsgqt/dot_general | solution.py:38
  39.5 0.0 slice-start
  39.5 5.9 %bitcast_reduce_fusion = (f32[16,2,4,8]{3,1,2,0:T(2,128)S(1)}, f32[16,4,4,128,2,8]{3,5,4,2,1,0:T(8,128)S(1)}) fusion(pred[16,4,128]{2,1,0:T(4,128)(4,1)S(1)} %broadcast_compare_fusion, bf16[16,2,4,8,128,1]{4,3,2,1,0,5:T(8,128)(2,1)S(1)} %get-tuple-element.12, bf16[16,4,4,128,128,1]{4,3,2,1,0,5:T(8,128)(2,1)} %bitcast.62), kind=kOutput, calls=%fused_computation.7 | convolution fusion | flops 135789568 | bytes 10760192 | tf_op jit(solution)/shard_map/rsgqd,rbgtd->rsgqbt/dot_general | solution.py:28
  45.5 0.3 fusion.18
  45.8 0.8 %fusion.5 = f32[16,2,4,8]{3,1,2,0:T(2,128)S(1)} fusion(f32[16,4,4,128,2,8]{3,5,4,2,1,0:T(8,128)S(1)} %get-tuple-element.28, f32[16,2,4,8]{3,1,2,0:T(2,128)S(1)} %max.11, pred[16,4,128]{2,1,0:T(4,128)(4,1)S(1)} %broadcast_compare_fusion), kind=kLoop, calls=%fused_computation.11 | loop fusion | flops 2096128 | bytes 2113536 | tf_op jit(solution)/shard_map/reduce_sum | solution.py:46
  46.7 1.6 %fusion.6 = f32[16,4,128,2,8]{2,4,3,1,0:T(8,128)S(1)} fusion(bf16[16,4,4,128,128,1]{4,3,2,1,0,5:T(8,128)(2,1)S(1)} %bitcast.61, f32[16,4,4,128,2,8]{3,5,4,2,1,0:T(8,128)S(1)} %get-tuple-element.28, f32[16,2,4,8]{3,1,2,0:T(2,128)S(1)} %add.110, f32[16,2,4,8]{3,1,2,0:T(2,128)S(1)} %max.11, pred[16,4,128]{2,1,0:T(4,128)(4,1)S(1)} %broadcast_compare_fusion), kind=kOutput, calls=%fused_computation.12 | convolution fusion | flops 136839168 | bytes 11026432 | tf_op jit(solution)/shard_map/rsgqbt,rbgtd->rsgqd/dot_general | solution.py:49
  48.3 0.3 fusion.10
  48.6 0.7 %copy.72 = bf16[16,2,4,8,128]{4,3,2,1,0:T(8,128)(2,1)} copy(bf16[16,2,4,8,128]{4,3,1,2,0:T(8,128)(2,1)S(1)} %fusion.10) | data formatting | bytes 524288 | tf_op jit(solution)/shard_map/convert_element_type | solution.py:55
  49.4 0.0 collective-permute-done.1
  49.4 1.1 %select_select_fusion.1 = bf16[4,4,128,128]{3,2,1,0:T(8,128)(2,1)} fusion(bf16[4,4,128,128]{3,2,1,0:T(8,128)(2,1)S(1)} %collective-permute-done.1, pred[4,128]{1,0:T(4,128)(4,1)S(1)} %get-tuple-element.20, pred[4,128]{1,0:T(4,128)(4,1)S(1)} %get-tuple-element.21, pred[4,128]{1,0:T(4,128)(4,1)S(1)} %get-tuple-element.19, ...), kind=kLoop, calls=%fused_computation.21 | loop fusion | flops 786432 | bytes 1052160 | tf_op jit(solution)/shard_map/jit(_where)/select_n | solution.py:67
  50.5 6.4 %collective-permute-done.2 = bf16[4,4,128,128]{3,2,1,0:T(8,128)(2,1)S(1)} collective-permute-done((bf16[4,4,128,128]{3,2,1,0:T(8,128)(2,1)}, bf16[4,4,128,128]{3,2,1,0:T(8,128)(2,1)S(1)}, u32[]{:S(2)}, u32[]{:S(2)}) %collective-permute-start.2) | collective-permute-done | bytes 524320 | tf_op jit(solution)/shard_map/ppermute | solution.py:16
  56.9 1.1 %select_select_fusion = bf16[4,4,128,128]{3,2,1,0:T(8,128)(2,1)} fusion(bf16[4,4,128,128]{3,2,1,0:T(8,128)(2,1)S(1)} %collective-permute-done.2, pred[4,128]{1,0:T(4,128)(4,1)S(1)} %get-tuple-element.20, pred[4,128]{1,0:T(4,128)(4,1)S(1)} %get-tuple-element.21, pred[4,128]{1,0:T(4,128)(4,1)S(1)} %get-tuple-element.19, ...), kind=kLoop, calls=%fused_computation.20 | loop fusion | flops 786432 | bytes 1052160 | tf_op jit(solution)/shard_map/jit(_where)/select_n | solution.py:67
  (26 shorter events, 0.1 us)
Async XLA Ops:
  1.4 36.6 %collective-permute-start = (bf16[1,2,40,128]{3,2,1,0:T(8,128)(2,1)S(1)}, bf16[1,2,40,128]{3,2,1,0:T(8,128)(2,1)S(1)}, u32[]{:S(2)}, u32[]{:S(2)}) collective-permute-start(bf16[1,2,40,128]{3,2,1,0:T(8,128)(2,1)S(1)} %pad_maximum_fusion), channel_id=1, source_target_pairs={{0,8},{2,10},{4,12},{6,14},{8,0},{10,2},{12,4},{14,6},{1,9},{3,11}... | collective-permute-start | bytes 61448 | tf_op jit(solution)/shard_map/ppermute | solution.py:16
  5.4 9.4 %copy-start.3 = (s32[16,4]{0,1:T(4,128)S(1)}, s32[16,4]{0,1:T(4,128)}, u32[]{:S(2)}) copy-start(s32[16,4]{0,1:T(4,128)} %param.13) | copy-start | bytes 772
  5.4 9.4 %copy-start.4 = (bf16[1,2,4,128]{3,2,1,0:T(4,128)(2,1)S(1)}, bf16[1,2,4,128]{3,2,1,0:T(4,128)(2,1)}, u32[]{:S(2)}) copy-start(bf16[1,2,4,128]{3,2,1,0:T(4,128)(2,1)} %param.20) | copy-start | bytes 6148
  5.4 9.5 %copy-start.5 = (bf16[1,2,4,128]{3,2,1,0:T(4,128)(2,1)S(1)}, bf16[1,2,4,128]{3,2,1,0:T(4,128)(2,1)}, u32[]{:S(2)}) copy-start(bf16[1,2,4,128]{3,2,1,0:T(4,128)(2,1)} %param.21) | copy-start | bytes 6148
  8.6 40.7 %collective-permute-start.1 = (bf16[4,4,128,128]{3,2,1,0:T(8,128)(2,1)}, bf16[4,4,128,128]{3,2,1,0:T(8,128)(2,1)S(1)}, u32[]{:S(2)}, u32[]{:S(2)}) collective-permute-start(bf16[4,4,128,128]{3,2,1,0:T(8,128)(2,1)} %get-tuple-element.7), channel_id=1, source_target_pairs={{0,8},{2,10},{4,12},{6,14},{8,0},{10,2},{12,4},{14,6},{1,9},{3,11}... | collective-permute-start | bytes 1572872 | tf_op jit(solution)/shard_map/ppermute | solution.py:16
  8.7 48.2 %collective-permute-start.2 = (bf16[4,4,128,128]{3,2,1,0:T(8,128)(2,1)}, bf16[4,4,128,128]{3,2,1,0:T(8,128)(2,1)S(1)}, u32[]{:S(2)}, u32[]{:S(2)}) collective-permute-start(bf16[4,4,128,128]{3,2,1,0:T(8,128)(2,1)} %get-tuple-element.8), channel_id=1, source_target_pairs={{0,8},{2,10},{4,12},{6,14},{8,0},{10,2},{12,4},{14,6},{1,9},{3,11}... | collective-permute-start | bytes 1572872 | tf_op jit(solution)/shard_map/ppermute | solution.py:16
  29.9 8.1 %copy-start = (bf16[16,2,32,128]{3,2,1,0:T(8,128)(2,1)S(1)}, bf16[16,2,32,128]{3,2,1,0:T(8,128)(2,1)}, u32[]{:S(2)}) copy-start(bf16[16,2,32,128]{3,2,1,0:T(8,128)(2,1)} %param.16) | copy-start | bytes 786436
  29.9 8.2 %copy-start.1 = (bf16[16,2,4,128]{3,2,1,0:T(4,128)(2,1)S(1)}, bf16[16,2,4,128]{3,2,1,0:T(4,128)(2,1)}, u32[]{:S(2)}) copy-start(bf16[16,2,4,128]{3,2,1,0:T(4,128)(2,1)} %param.18) | copy-start | bytes 98308
  29.9 8.2 %copy-start.2 = (bf16[16,2,4,128]{3,2,1,0:T(4,128)(2,1)S(1)}, bf16[16,2,4,128]{3,2,1,0:T(4,128)(2,1)}, u32[]{:S(2)}) copy-start(bf16[16,2,4,128]{3,2,1,0:T(4,128)(2,1)} %param.17) | copy-start | bytes 98308
  39.5 7.1 %slice-start = ((s8[8388608]{0:T(1024)(128)(4,1)}), s8[4194304]{0:T(1024)(128)(4,1)S(1)}, s32[]{:S(2)}) async-start(s8[8388608]{0:T(1024)(128)(4,1)} %bitcast.59), calls=%async_computation | async-start | bytes 8388608
  39.5 7.1 %slice-start.1 = ((s8[8388608]{0:T(1024)(128)(4,1)}), s8[4194304]{0:T(1024)(128)(4,1)S(1)}, s32[]{:S(2)}) async-start(s8[8388608]{0:T(1024)(128)(4,1)} %bitcast.59), calls=%async_computation.1 | async-start | bytes 8388608

commit v3 on v2

--- a/solution.py
+++ b/solution.py
@@ -16,43 +16,128 @@
     return lax.ppermute(value, axis, pairs)
 
 
-def attend_batch(key_blocks, value_blocks, length, query_tokens, recent_keys, recent_values):
+def attend_kernel(
+    lengths_ref, table_ref, key_ref, value_ref, query_ref, recent_key_ref, recent_value_ref, out_ref,
+    keys, values, recent_scores, sems,
+):
+    kv_count, block_len, head_width = key_ref.shape[1:]
+    block_count, row_count = table_ref.shape
+    token_rows = query_ref.shape[1] // row_count
+    step_count = recent_key_ref.shape[1] // row_count
+    group_size = token_rows // step_count
+    score_scale = 1.0 / math.sqrt(head_width)
+    own_index = lax.axis_index("inst")
+
+    def copies(row, block):
+        place = table_ref[block, row]
+        return (
+            pltpu.make_async_copy(key_ref.at[place], keys.at[place], sems.at[0, block, row]),
+            pltpu.make_async_copy(value_ref.at[place], values.at[place], sems.at[1, block, row]),
+        )
+
+    @pl.loop(0, row_count)
+    def _(row):
+        for block in range(block_count):
+
+            @pl.when(block * block_len < lengths_ref[own_index, row])
+            def _():
+                for copy in copies(row, block):
+                    copy.start()
+
+    contract_last = (((1,), (1,)), ((), ()))
+    rows = lax.broadcasted_iota(jnp.int32, recent_scores.shape[1:], 0)
+    columns = lax.broadcasted_iota(jnp.int32, recent_scores.shape[1:], 1)
+    step = (rows % token_rows) // group_size
+    seen = (rows // token_rows == columns // step_count) & (columns % step_count <= step)
+    for head in range(kv_count):
+        products = lax.dot_general(
+            query_ref[head], recent_key_ref[head], contract_last, preferred_element_type=jnp.float32
+        )
+        recent_scores[head] = jnp.where(seen, products * score_scale, masked_score)
+
+    @pl.loop(0, row_count)
+    def _(row):
+        length = lengths_ref[own_index, row]
+        own_rows = pl.ds(pl.multiple_of(row * token_rows, token_rows), token_rows)
+
+        def attend(used):
+            places = [table_ref[block, row] for block in range(used)]
+            for block in range(used):
+                for copy in copies(row, block):
+                    copy.wait()
+            for head in range(kv_count):
+                query = query_ref[head, own_rows, :]
+                scores = []
+                for block in range(used):
+                    products = lax.dot_general(
+                        query,
+                        keys[places[block], head],
+                        contract_last,
+                        preferred_element_type=jnp.float32,
+                    )
+                    scores.append(products * score_scale)
+                position = lax.broadcasted_iota(jnp.int32, scores[-1].shape, 1) + (used - 1) * block_len
+                scores[-1] = jnp.where(position < length, scores[-1], masked_score)
+                scores = jnp.concatenate(scores, axis=1)
+                recent = recent_scores[head, own_rows, :]
+                highest = jnp.maximum(
+                    jnp.max(scores, axis=1, keepdims=True), jnp.max(recent, axis=1, keepdims=True)
+                )
+                weight = jnp.exp(scores - highest)
+                recent_weight = jnp.exp(recent - highest)
+                denominator = jnp.sum(weight, axis=1, keepdims=True) + jnp.sum(
+                    recent_weight, axis=1, keepdims=True
+                )
+                weight = (weight / denominator).astype(jnp.bfloat16)
+                recent_weight = (recent_weight / denominator).astype(jnp.bfloat16)
+                total = jnp.dot(
+                    recent_weight, recent_value_ref[head], preferred_element_type=jnp.float32
+                )
+                for block in range(used):
+                    total += jnp.dot(
+                        weight[:, block * block_len : (block + 1) * block_len],
+                        values[places[block], head],
+                        preferred_element_type=jnp.float32,
+                    )
+                out_ref[head, own_rows, :] = total.astype(out_ref.dtype)
+
+        for used in range(1, block_count + 1):
+            pl.when((length + block_len - 1) // block_len == used)(lambda used=used: attend(used))
+
+
+def attend_rows(key_pool, value_pool, block_table, lengths, query_tokens, recent_keys, recent_values):
     row_count, step_count, head_count, head_width = query_tokens.shape
-    kv_count = key_blocks.shape[2]
+    kv_count = key_pool.shape[1]
     group_size = head_count // kv_count
-    block_count = key_blocks.shape[1]
-    block_len = key_blocks.shape[3]
-    score_scale = 1.0 / math.sqrt(head_width)
+    block_count = block_table.shape[1]
     grouped = query_tokens.reshape(row_count, step_count, kv_count, group_size, head_width)
-    context = (
-        jnp.einsum("rsgqd,rbgtd->rsgqbt", grouped, key_blocks, preferred_element_type=jnp.float32)
-        * score_scale
-    )
-    position = (
-        jnp.arange(block_count, dtype=jnp.int32)[:, None] * block_len
-        + jnp.arange(block_len, dtype=jnp.int32)[None, :]
-    )
-    valid = position[None] < length[:, None, None]
-    context = jnp.where(valid[:, None, None, None], context, masked_score)
-    recent = (
-        jnp.einsum("rsgqd,rtgd->rsgqt", grouped, recent_keys, preferred_element_type=jnp.float32)
-        * score_scale
-    )
-    causal = jnp.arange(step_count)[None, :] <= jnp.arange(step_count)[:, None]
-    recent = jnp.where(causal[None, :, None, None, :], recent, masked_score)
-    highest = jnp.maximum(jnp.max(context, axis=(4, 5)), jnp.max(recent, axis=4))
-    context_exp = jnp.exp(context - highest[..., None, None])
-    recent_exp = jnp.exp(recent - highest[..., None])
-    denominator = jnp.sum(context_exp, axis=(4, 5)) + jnp.sum(recent_exp, axis=4)
-    context_weight = (context_exp / denominator[..., None, None]).astype(jnp.bfloat16)
-    recent_weight = (recent_exp / denominator[..., None]).astype(jnp.bfloat16)
-    result_sum = jnp.einsum(
-        "rsgqbt,rbgtd->rsgqd", context_weight, value_blocks, preferred_element_type=jnp.float32
-    )
-    result_sum = result_sum + jnp.einsum(
-        "rsgqt,rtgd->rsgqd", recent_weight, recent_values, preferred_element_type=jnp.float32
-    )
-    return result_sum.astype(jnp.bfloat16).reshape(row_count, step_count, head_count, head_width)
+    grouped = grouped.transpose(2, 0, 1, 3, 4).reshape(kv_count, -1, head_width)
+    recent_keys = recent_keys.transpose(2, 0, 1, 3).reshape(kv_count, -1, head_width)
+    recent_values = recent_values.transpose(2, 0, 1, 3).reshape(kv_count, -1, head_width)
+    smem = pl.BlockSpec(memory_space=pltpu.SMEM)
+    vmem = pl.BlockSpec(memory_space=pltpu.VMEM)
+    pool = pl.BlockSpec(memory_space=pltpu.HBM)
+    out = pl.pallas_call(
+        attend_kernel,
+        out_shape=jax.ShapeDtypeStruct(grouped.shape, grouped.dtype),
+        in_specs=[smem, smem, pool, pool, vmem, vmem, vmem],
+        out_specs=vmem,
+        scratch_shapes=[
+            pltpu.VMEM(key_pool.shape, key_pool.dtype),
+            pltpu.VMEM(value_pool.shape, value_pool.dtype),
+            pltpu.VMEM(grouped.shape[:2] + recent_keys.shape[1:2], jnp.float32),
+            pltpu.SemaphoreType.DMA((2, block_count, row_count)),
+        ],
+        compiler_params=pltpu.CompilerParams(vmem_limit_bytes=24 * 1024 * 1024),
+        cost_estimate=pl.CostEstimate(
+            flops=4 * grouped.size * block_count * key_pool.shape[2],
+            bytes_accessed=2 * key_pool.size * 2,
+            transcendentals=grouped.size * block_count,
+        ),
+        name="attend",
+    )(lengths, block_table.T, key_pool, value_pool, grouped, recent_keys, recent_values)
+    out = out.reshape(kv_count, row_count, step_count, group_size, head_width)
+    return out.transpose(1, 2, 0, 3, 4).reshape(query_tokens.shape)
 
 
 def guest_block(blocks, length, recent_rows):
@@ -121,6 +206,7 @@
     got_keys = passed_along(send_keys, "inst", half_cycle)
     got_values = passed_along(send_values, "inst", half_cycle)
     guest_tokens = jnp.concatenate([guest_queries, guest_new_keys, guest_new_values], axis=2)
+    guest_tokens, send_keys = lax.optimization_barrier((guest_tokens, send_keys))
     moved_tokens = passed_along(guest_tokens, "inst", half_cycle)
     head_count = queries.shape[2]
     kv_count = new_keys.shape[2]
@@ -134,10 +220,11 @@
     moved_length = lax.dynamic_index_in_dim(source_lengths, request, 0, keepdims=False)
     row_ids = jnp.arange(own_lengths.shape[0], dtype=jnp.int32)
     replace = ((source == own_index) & (row_ids == request))[:, None, None, None]
-    attended = attend_batch(
-        key_pool[block_table],
-        value_pool[block_table],
-        own_lengths,
+    attended = attend_rows(
+        key_pool,
+        value_pool,
+        block_table,
+        lengths,
         jnp.where(replace, moved_tokens[:, :, :head_count], queries),
         jnp.where(replace, moved_tokens[:, :, head_count : head_count + kv_count], new_keys),
         jnp.where(replace, moved_tokens[:, :, head_count + kv_count :], new_values),

time: 58.4 us -> 89.2 us (1.53)
  Pallas kernels: 3.19 us -> 39.9 us
  waiting for transfers between devices: 6.45 us -> 24.8 us
  local copies, waits for them, and re-layouts: 20.4 us -> 7.78 us
  matrix products: 9.19 us -> 0 us
  other arithmetic: 5.16 us -> 3.07 us
    pallas_call x0 -> x1, Pallas kernels: none -> 36.7 us  [attend_rows(): pl.pallas_call(attend_kernel, out_shape=jax.ShapeDtypeStruct(grouped.shap...]
    ppermute x3, waiting for transfers between devices: 6.45 us -> 24.8 us  [passed_along(): return lax.ppermute(value, axis, pairs)]
    gather x2 -> x0, local copies, waits for them, and re-layouts: 16.1 us -> none  [the longest x1 8.06 us: shards(): value_pool[block_table]]
    dot_general x4 -> x0, matrix products: 9.19 us -> none  [the longest x1 5.94 us: attend_batch(): jnp.einsum('rsgqd,rbgtd->rsgqbt', grouped, key_blocks, preferred_element_...]
    unnamed x16 -> x20, local copies, waits for them, and re-layouts: 0.03 us -> 5 us
    reduce_sum x2 -> x0, other arithmetic: 1.08 us -> none  [the longest x1 0.82 us: attend_batch(): jnp.sum(context_exp, axis=(4, 5)) + jnp.sum(recent_exp, axis=4)]
  transfers between devices with their start and end apart: 3 -> 3, of which waited for: 1 -> 1; matrix products, arithmetic and copies ran while one was open for 57% -> 5% of each run, Pallas kernels for 6% -> 41%
where the time goes in v3:
time: 89.2 us; the launch traced here: 89.3 us
  Pallas kernels  39.9 us (45%)
  waiting for transfers between devices  24.8 us (28%)
  local copies, waits for them, and re-layouts  7.78 us (9%)
  starting transfers between devices  7.09 us (8%)
  between operations  6.63 us (7%)
  other arithmetic  3.07 us (3%)
    pallas_call x1, Pallas kernels, attend_rows(): pl.pallas_call(attend_kernel, out_shape=jax.ShapeDtypeStruct(grouped.shap...  36.7 us
    ppermute x3, waiting for transfers between devices, passed_along(): return lax.ppermute(value, axis, pairs)  24.8 us
    ppermute x3, starting transfers between devices, passed_along(): return lax.ppermute(value, axis, pairs)  7.09 us
    unnamed x20, local copies, waits for them, and re-layouts  5 us
    pallas_call x1, Pallas kernels, pick_moved(): pl.pallas_call(lambda *refs: pick_kernel(blocks, half_cycle, *refs), out_...  3.2 us
    select_n x2, other arithmetic, guest_block(): jnp.where(position == length + step_index, recent_rows[step_index][None,...  2.13 us
  transfers between devices with their start and end apart: 3, of which 1 were waited for; matrix products, arithmetic and copies ran while one was open for 5% of the time, Pallas kernels for 41%

profile of v3, /device:TPU:0, one launch (start us, length us, event | category | flops | bytes accessed | tf_op | source)
XLA Modules:
  0.0 89.3 jit_solution(8639922955179262457)
XLA Ops:
  0.6 0.0 copy-start.7
  0.6 0.0 copy-start.8
  0.7 0.0 copy-start.9
  0.7 0.0 copy-start.3
  0.7 0.0 copy-start.4
  0.7 0.0 copy-start.5
  0.7 0.0 copy-start.6
  0.7 0.0 copy-start.2
  0.7 3.2 %pick_moved.1 = (bf16[4,4,128,128]{3,2,1,0:T(8,128)(2,1)}, bf16[4,4,128,128]{3,2,1,0:T(8,128)(2,1)}) custom-call(s32[4,3]{1,0:T(4,128)} %refs_0_.1, s32[4,16]{1,0:T(4,128)} %bitcast.40, bf16[40,4,128,128]{3,2,1,0:T(8,128)(2,1)} %key_ref.1, bf16[40,4,128,128]{3,2,1,0:T(8,128)(2,1)} %value_ref.1), custom_call_target="tpu_custom_call" | custom-call | tf_op jit(solution)/shard_map/pick_moved/pallas_call | solution.py:180
  3.9 4.1 %collective-permute-start.1 = (bf16[4,4,128,128]{3,2,1,0:T(8,128)(2,1)}, bf16[4,4,128,128]{3,2,1,0:T(8,128)(2,1)S(1)}, u32[]{:S(2)}, u32[]{:S(2)}) collective-permute-start(bf16[4,4,128,128]{3,2,1,0:T(8,128)(2,1)} %get-tuple-element.8), channel_id=1, source_target_pairs={{0,8},{2,10},{4,12},{6,14},{8,0},{10,2},{12,4},{14,6},{1,9},{3,11}... | collective-permute-start | bytes 1572872 | tf_op jit(solution)/shard_map/ppermute | solution.py:16
  8.0 0.0 copy-done.7
  8.0 0.0 copy-done.8
  8.0 0.0 copy-done.9
  8.0 0.1 collective-permute-start
  8.1 2.9 %collective-permute-start.2 = (bf16[4,4,128,128]{3,2,1,0:T(8,128)(2,1)}, bf16[4,4,128,128]{3,2,1,0:T(8,128)(2,1)S(1)}, u32[]{:S(2)}, u32[]{:S(2)}) collective-permute-start(bf16[4,4,128,128]{3,2,1,0:T(8,128)(2,1)} %get-tuple-element.10), channel_id=1, source_target_pairs={{0,8},{2,10},{4,12},{6,14},{8,0},{10,2},{12,4},{14,6},{1,9},{3,11}... | collective-permute-start | bytes 1572872 | tf_op jit(solution)/shard_map/ppermute | solution.py:16
  11.0 0.7 constant_dynamic-slice_fusion
  11.7 0.6 fusion.3
  17.5 0.6 dynamic_slice.11
  18.8 0.1 fusion.2
  18.8 0.7 compare_and_fusion
  19.5 24.8 %collective-permute-done = bf16[1,2,40,128]{3,2,1,0:T(8,128)(2,1)S(1)} collective-permute-done((bf16[1,2,40,128]{3,2,1,0:T(8,128)(2,1)S(1)}, bf16[1,2,40,128]{3,2,1,0:T(8,128)(2,1)S(1)}, u32[]{:S(2)}, u32[]{:S(2)}) %collective-permute-start) | collective-permute-done | bytes 20512 | tf_op jit(solution)/shard_map/ppermute | solution.py:16
  44.3 0.1 select_bitcast_fusion
  44.5 0.1 select_bitcast_fusion.1
  44.7 0.0 copy-start
  44.7 2.5 %copy-done = bf16[40,4,128,128]{3,2,1,0:T(8,128)(2,1)S(1)} copy-done((bf16[40,4,128,128]{3,2,1,0:T(8,128)(2,1)S(1)}, bf16[40,4,128,128]{3,2,1,0:T(8,128)(2,1)}, u32[]{:S(2)}) %copy-start) | copy-done | bytes 5242904
  47.2 2.5 %copy-done.1 = bf16[40,4,128,128]{3,2,1,0:T(8,128)(2,1)S(1)} copy-done((bf16[40,4,128,128]{3,2,1,0:T(8,128)(2,1)S(1)}, bf16[40,4,128,128]{3,2,1,0:T(8,128)(2,1)}, u32[]{:S(2)}) %copy-start.1) | copy-done | bytes 5242904
  49.7 36.7 %attend.1 = bf16[4,256,128]{2,1,0:T(8,128)(2,1)S(1)} custom-call(s32[8,16]{1,0:T(8,128)S(1)} %copy-done.3, s32[4,16]{1,0:T(4,128)S(1)} %bitcast.41, bf16[40,4,128,128]{3,2,1,0:T(8,128)(2,1)S(1)} %copy-done, bf16[40,4,128,128]{3,2,1,0:T(8,128)(2,1)S(1)} %copy-done.1, bf16[4,256,128]{2,1,0:T(8,128)(2,1)S(1)} %bitcast.36, bf16[4,32,128]{2,1,0:T(8,128)(2,1)S(1)} %bitcast.38, ...), custom_call_target="tpu_custom_call" | custom-call | flops 268435456 | bytes 10485760 | tf_op jit(solution)/shard_map/attend/pallas_call | solution.py:120
  86.3 0.8 copy.19
  87.1 0.0 collective-permute-done.1
  87.1 1.1 %select_select_fusion.1 = bf16[4,4,128,128]{3,2,1,0:T(8,128)(2,1)} fusion(bf16[4,4,128,128]{3,2,1,0:T(8,128)(2,1)S(1)} %collective-permute-done.1, pred[4,128]{1,0:T(4,128)(4,1)S(1)} %get-tuple-element.20, pred[4,128]{1,0:T(4,128)(4,1)S(1)} %get-tuple-element.21, pred[4,128]{1,0:T(4,128)(4,1)S(1)} %get-tuple-element.19, ...), kind=kLoop, calls=%fused_computation.1 | loop fusion | flops 786432 | bytes 1052160 | tf_op jit(solution)/shard_map/jit(_where)/select_n | solution.py:152
  88.2 0.0 collective-permute-done.2
  88.2 1.1 %select_select_fusion = bf16[4,4,128,128]{3,2,1,0:T(8,128)(2,1)} fusion(bf16[4,4,128,128]{3,2,1,0:T(8,128)(2,1)S(1)} %collective-permute-done.2, pred[4,128]{1,0:T(4,128)(4,1)S(1)} %get-tuple-element.20, pred[4,128]{1,0:T(4,128)(4,1)S(1)} %get-tuple-element.21, pred[4,128]{1,0:T(4,128)(4,1)S(1)} %get-tuple-element.19, bf16[4,128]{1,0:T(4,128)(2,1)S(1)} %get-tuple-element.16, ...), kind=kLoop, calls=%fused_computation | loop fusion | flops 786432 | bytes 1052160 | tf_op jit(solution)/shard_map/jit(_where)/select_n | solution.py:152
  (15 shorter events, 0.1 us)
Async XLA Ops:
  0.6 7.4 %copy-start.7 = (bf16[1,2,32,128]{3,2,1,0:T(8,128)(2,1)S(1)}, bf16[1,2,32,128]{3,2,1,0:T(8,128)(2,1)}, u32[]{:S(2)}) copy-start(bf16[1,2,32,128]{3,2,1,0:T(8,128)(2,1)} %param.19) | copy-start | bytes 49156
  0.6 7.4 %copy-start.8 = (bf16[1,2,4,128]{3,2,1,0:T(4,128)(2,1)S(1)}, bf16[1,2,4,128]{3,2,1,0:T(4,128)(2,1)}, u32[]{:S(2)}) copy-start(bf16[1,2,4,128]{3,2,1,0:T(4,128)(2,1)} %param.20) | copy-start | bytes 6148
  0.7 7.4 %copy-start.9 = (bf16[1,2,4,128]{3,2,1,0:T(4,128)(2,1)S(1)}, bf16[1,2,4,128]{3,2,1,0:T(4,128)(2,1)}, u32[]{:S(2)}) copy-start(bf16[1,2,4,128]{3,2,1,0:T(4,128)(2,1)} %param.21) | copy-start | bytes 6148
  0.7 16.8 %copy-start.3 = (s32[8,16]{1,0:T(8,128)S(1)}, s32[8,16]{1,0:T(8,128)}, u32[]{:S(2)}) copy-start(s32[8,16]{1,0:T(8,128)} %lengths_ref.1) | copy-start | bytes 1540
  0.7 43.7 %copy-start.4 = (bf16[16,2,32,128]{3,2,1,0:T(8,128)(2,1)S(1)}, bf16[16,2,32,128]{3,2,1,0:T(8,128)(2,1)}, u32[]{:S(2)}) copy-start(bf16[16,2,32,128]{3,2,1,0:T(8,128)(2,1)} %param.16) | copy-start | bytes 786436
  0.7 43.8 %copy-start.5 = (bf16[16,2,4,128]{3,2,1,0:T(4,128)(2,1)S(1)}, bf16[16,2,4,128]{3,2,1,0:T(4,128)(2,1)}, u32[]{:S(2)}) copy-start(bf16[16,2,4,128]{3,2,1,0:T(4,128)(2,1)} %param.18) | copy-start | bytes 98308
  0.7 43.8 %copy-start.6 = (bf16[16,2,4,128]{3,2,1,0:T(4,128)(2,1)S(1)}, bf16[16,2,4,128]{3,2,1,0:T(4,128)(2,1)}, u32[]{:S(2)}) copy-start(bf16[16,2,4,128]{3,2,1,0:T(4,128)(2,1)} %param.17) | copy-start | bytes 98308
  0.7 44.0 %copy-start.2 = (s32[16,4]{0,1:T(4,128)S(1)}, s32[16,4]{0,1:T(4,128)}, u32[]{:S(2)}) copy-start(s32[16,4]{0,1:T(4,128)} %param.13) | copy-start | bytes 772
  3.9 83.2 %collective-permute-start.1 = (bf16[4,4,128,128]{3,2,1,0:T(8,128)(2,1)}, bf16[4,4,128,128]{3,2,1,0:T(8,128)(2,1)S(1)}, u32[]{:S(2)}, u32[]{:S(2)}) collective-permute-start(bf16[4,4,128,128]{3,2,1,0:T(8,128)(2,1)} %get-tuple-element.8), channel_id=1, source_target_pairs={{0,8},{2,10},{4,12},{6,14},{8,0},{10,2},{12,4},{14,6},{1,9},{3,11}... | collective-permute-start | bytes 1572872 | tf_op jit(solution)/shard_map/ppermute | solution.py:16
  8.0 36.3 %collective-permute-start = (bf16[1,2,40,128]{3,2,1,0:T(8,128)(2,1)S(1)}, bf16[1,2,40,128]{3,2,1,0:T(8,128)(2,1)S(1)}, u32[]{:S(2)}, u32[]{:S(2)}) collective-permute-start(bf16[1,2,40,128]{3,2,1,0:T(8,128)(2,1)S(1)} %pad_maximum_fusion), channel_id=1, source_target_pairs={{0,8},{2,10},{4,12},{6,14},{8,0},{10,2},{12,4},{14,6},{1,9},{3,11}... | collective-permute-start | bytes 61448 | tf_op jit(solution)/shard_map/ppermute | solution.py:16
  8.1 80.0 %collective-permute-start.2 = (bf16[4,4,128,128]{3,2,1,0:T(8,128)(2,1)}, bf16[4,4,128,128]{3,2,1,0:T(8,128)(2,1)S(1)}, u32[]{:S(2)}, u32[]{:S(2)}) collective-permute-start(bf16[4,4,128,128]{3,2,1,0:T(8,128)(2,1)} %get-tuple-element.10), channel_id=1, source_target_pairs={{0,8},{2,10},{4,12},{6,14},{8,0},{10,2},{12,4},{14,6},{1,9},{3,11}... | collective-permute-start | bytes 1572872 | tf_op jit(solution)/shard_map/ppermute | solution.py:16
  44.7 2.5 %copy-start = (bf16[40,4,128,128]{3,2,1,0:T(8,128)(2,1)S(1)}, bf16[40,4,128,128]{3,2,1,0:T(8,128)(2,1)}, u32[]{:S(2)}) copy-start(bf16[40,4,128,128]{3,2,1,0:T(8,128)(2,1)} %key_ref.1) | copy-start | bytes 15728644
  47.2 2.5 %copy-start.1 = (bf16[40,4,128,128]{3,2,1,0:T(8,128)(2,1)S(1)}, bf16[40,4,128,128]{3,2,1,0:T(8,128)(2,1)}, u32[]{:S(2)}) copy-start(bf16[40,4,128,128]{3,2,1,0:T(8,128)(2,1)} %value_ref.1) | copy-start | bytes 15728644
